TPU v7x, 32 devices: a whole 2x2x4 slice. The times are simulated.
32 devices in a mesh: groups: 2 (over x), rows: 8 (over z, y), wide: 2 (over core).
Axes of the slice: x: 2, y: 2, z: 4, core: 2. Of those that a mesh axis runs over, the one named last changes fastest.
Arguments:
- activations: bfloat16 [8192, 3584], P(('groups', 'rows')), parts along dimension 0
- cotangents: bfloat16 [8192, 2560], P(('groups', 'rows'), 'wide'), parts along dimension 0
- left_root: float32 [7168, 3584], P(('groups', 'rows')), parts along dimension 0, as said below
- right_root: float32 [4, 1280, 1280], P(('groups', 'wide')), parts along dimension 0, as said below
- momentum: float32 [7168, 2560], P(('groups', 'rows'), 'wide'), parts along dimension 0, may hold values from -6 to 6
- second_moment: float32 [7168, 2560], P(('groups', 'rows'), 'wide'), parts along dimension 0, may hold values from 0.25 to 1
Outputs:
- new_momentum: float32 [7168, 2560], P(('groups', 'rows'), 'wide'), parts along dimension 0
- new_second: float32 [7168, 2560], P(('groups', 'rows'), 'wide'), parts along dimension 0
There are 2 independent parts, one for each index of `groups`. A program takes and returns all parts, laid end to end along the dimension named above; each array names one. Nothing has to cross between parts.
Inputs may be any that keep to these rules, and one draw needn't show every extreme that they name: left_root is symmetric positive definite. Each block right_root[w] is symmetric positive definite.
All inputs are finite; a program needn't handle non-finite values.
Results may differ from a plain program's by a relative error of at most 0.01.
Values may be sent and summed in bfloat16 or wider, within the bound.
A program may use at most 192 MiB of HBM per device.

v0:
```python
import jax
import jax.numpy as jnp
from jax import lax
from jax.sharding import PartitionSpec as P

BETA_ONE = 0.9
BETA_TWO = 0.99
GRAFT_EPS = 1e-08
NORM_EPS = 1e-06


def per_device(activations, cotangents, left_root, right_root, momentum, second_moment):
    partial_term = lax.dot_general(
        activations, cotangents, (((0,), (0,)), ((), ())), preferred_element_type=jnp.float32
    )
    gradient = lax.psum_scatter(
        lax.optimization_barrier(partial_term.astype(jnp.bfloat16))
        .astype(jnp.float32)
        .astype(jnp.bfloat16),
        "rows",
        scatter_dimension=0,
        tiled=True,
    ).astype(jnp.float32)
    new_second = BETA_TWO * second_moment + (1.0 - BETA_TWO) * gradient * gradient
    direction = gradient / (jnp.sqrt(new_second) + GRAFT_EPS)
    graft_local = jnp.sum(direction * direction)
    graft_total = lax.psum(graft_local, "rows")
    rounded_gradient = lax.optimization_barrier(gradient.astype(jnp.bfloat16))
    left_product = jnp.dot(
        left_root,
        lax.all_gather(rounded_gradient, "rows", axis=0, tiled=True).astype(jnp.float32),
        precision=lax.Precision.HIGHEST,
        preferred_element_type=jnp.float32,
    )
    preconditioned = jnp.dot(
        left_product,
        right_root[0],
        precision=lax.Precision.HIGHEST,
        preferred_element_type=jnp.float32,
    )
    root_local = jnp.sum(preconditioned * preconditioned)
    root_total = lax.psum(root_local, "rows")
    factor = jnp.sqrt(graft_total) / jnp.sqrt(root_total + NORM_EPS)
    new_momentum = BETA_ONE * momentum + factor * preconditioned
    return (new_momentum, new_second)


def solution(mesh):
    placed = (
        P(("groups", "rows"), None),
        P(("groups", "rows"), "wide"),
        P(("groups", "rows"), None),
        P(("groups", "wide"), None, None),
        P(("groups", "rows"), "wide"),
        P(("groups", "rows"), "wide"),
    )
    return jax.shard_map(
        per_device,
        mesh=mesh,
        in_specs=placed,
        out_specs=(P(("groups", "rows"), "wide"), P(("groups", "rows"), "wide")),
        check_vma=False,
    )
```

profile of v0, /device:TPU:0, one launch (start us, length us, event | category | flops | bytes accessed | tf_op | source)
XLA Modules:
  0.0 385.0 jit_solution(9953570475160754250)
XLA Ops:
  7.2 0.0 copy-start
  7.2 0.0 reduce-scatter.2.cloned.1.call-start
  7.2 1.3 copy-done
  8.5 10.4 %convolution_convert_fusion = bf16[3584,1280]{1,0:T(8,128)(2,1)} fusion(bf16[512,3584]{1,0:T(8,128)(2,1)} %param.6, bf16[512,1280]{1,0:T(8,128)(2,1)S(1)} %copy-done), kind=kOutput, calls=%fused_computation | convolution fusion | flops 4702208000 | bytes 14155776 | tf_op jit(solution)/shard_map/dot_general | solution.py:13
  18.9 0.0 reduce-scatter.2.cloned.1.call-update
  18.9 0.2 all-gather.2.cloned.1.call-start
  19.1 162.8 %reduce-scatter.2.cloned.1.call-done = bf16[448,1280]{1,0:T(8,128)(2,1)} async-done(((bf16[3584,1280]{1,0:T(8,128)(2,1)}), bf16[448,1280]{1,0:T(8,128)(2,1)}) %reduce-scatter.2.cloned.1.call-update) | async-done | bytes 1146896 | tf_op jit(solution)/shard_map/reduce_scatter | solution.py:16
  181.9 0.0 all-gather.2.cloned.1.call-update
  181.9 5.2 %fusion.4 = (f32[]{:T(128)}, f32[448,1280]{1,0:T(8,128)}) fusion(bf16[448,1280]{1,0:T(8,128)(2,1)} %reduce-scatter.2.cloned.1.call-done, f32[448,1280]{1,0:T(8,128)} %param.11), kind=kLoop, calls=%fused_computation.9 | loop fusion | flops 5160959 | bytes 5734404 | tf_op jit(solution)/shard_map/reduce_sum | solution.py:26
  187.1 131.2 %all-gather.2.cloned.1.call-done = bf16[3584,1280]{1,0:T(8,128)(2,1)} async-done(((bf16[448,1280]{1,0:T(8,128)(2,1)}), bf16[3584,1280]{1,0:T(8,128)(2,1)}) %all-gather.2.cloned.1.call-update) | async-done | bytes 9175056 | tf_op jit(solution)/shard_map/all_gather | solution.py:31
  318.3 21.1 %fusion.6 = f32[1280,448]{1,0:T(8,128)S(1)} fusion(bf16[3584,1280]{1,0:T(8,128)(2,1)} %all-gather.2.cloned.1.call-done, f32[448,3584]{1,0:T(8,128)} %param.8), kind=kOutput, calls=%fused_computation.10 | convolution fusion | flops 24662507520 | bytes 17891328 | tf_op jit(solution)/shard_map/dot_general | solution.py:29
  339.4 14.4 %multiply_reduce_fusion = (f32[]{:T(128)}, f32[448,1280]{1,0:T(8,128)}) fusion(f32[1280,448]{1,0:T(8,128)S(1)} %fusion.6, f32[1,1280,1280]{2,1,0:T(8,128)} %param.9), kind=kOutput, calls=%fused_computation.8 | convolution fusion | flops 8809185280 | bytes 11141124 | tf_op jit(solution)/shard_map/dot_general | solution.py:35
  353.7 19.1 %all-reduce = (f32[]{:T(128)}, f32[]{:T(128)}) all-reduce(f32[]{:T(128)} %get-tuple-element.4, f32[]{:T(128)} %get-tuple-element.6), channel_id=1, replica_groups=mesh['groups'=2,'rows'=8,'wide'=2] {'rows'}, use_global_device_ids=true, to_apply=%region_2.0 | all-reduce | flops 2 | bytes 16 | tf_op jit(solution)/shard_map/psum | solution.py:27
  374.1 4.0 %multiply_add_fusion = f32[448,1280]{1,0:T(8,128)} fusion(f32[448,1280]{1,0:T(8,128)} %get-tuple-element.7, f32[448,1280]{1,0:T(8,128)} %param.10, f32[]{:T(128)S(6)} %div.7), kind=kLoop, calls=%fused_computation.7 | loop fusion | flops 1720320 | bytes 6881284 | tf_op jit(solution)/shard_map/add | solution.py:44
Async XLA Ops:
  7.2 1.3 copy-start
  7.2 174.7 %reduce-scatter.2.cloned.1.call-start = ((), (), s32[]{:S(2)}) async-start(), calls=%async_computation.1 | async-start | bytes 10321920 | tf_op jit(solution)/shard_map/reduce_scatter | solution.py:16
  18.9 299.4 %all-gather.2.cloned.1.call-start = ((), (), s32[]{:S(2)}) async-start(), calls=%async_computation.2 | async-start | bytes 10321920 | tf_op jit(solution)/shard_map/all_gather | solution.py:31
Sparse Core Ops, SparseCore 0:
  19.0 162.8 reduce-scatter.1
  184.3 133.9 all-gather.1
where the time goes:
time: 385 us
  waiting for transfers between devices  294 us (76%)
  matrix products  45.8 us (12%)
  blocking collectives  19.1 us (5%)
  between operations  15.3 us (4%)
  other arithmetic  9.22 us (2%)
    reduce_scatter x1, waiting for transfers between devices, per_device(): lax.psum_scatter(lax.optimization_barrier(partial_term.astype(jnp.bfloat1...  163 us
    all_gather x1, waiting for transfers between devices, per_device(): lax.all_gather(rounded_gradient, 'rows', axis=0, tiled=True)  131 us
    dot_general x1, matrix products, per_device(): jnp.dot(left_root, lax.all_gather(rounded_gradient, 'rows', axis=0, tiled...  21.1 us
    psum x1, blocking collectives, per_device(): graft_total = lax.psum(graft_local, 'rows')  19.1 us
    dot_general x1, matrix products, per_device(): jnp.dot(left_product, right_root[0], precision=lax.Precision.HIGHEST, pre...  14.4 us
    dot_general x1, matrix products, per_device(): lax.dot_general(activations, cotangents, (((0,), (0,)), ((), ())), prefer...  10.4 us
  transfers between devices with their start and end apart: 2, of which 2 were waited for; matrix products, arithmetic and copies ran while one was open for 1% of the time, Pallas kernels for 0%

commit v1 on v0

v1 whole, which is shorter than its diff:
```python
import functools

import jax
import jax.numpy as jnp
from jax import lax
from jax.experimental import pallas as pl
from jax.experimental.pallas import tpu as pltpu
from jax.sharding import PartitionSpec as P

BETA_ONE = 0.9
BETA_TWO = 0.99
GRAFT_EPS = 1e-08
NORM_EPS = 1e-06
CW = 256
MESH = pl.DeviceIdType.MESH
F32 = jnp.float32
BF16 = jnp.bfloat16


def kernel(
    n, wides, m, nc, blk, tok,
    at_in, c_in, l2, r_in, second,
    pre, g_out, tot,
    at2, cc, rbuf, lbuf, gbuf, lown, lr, pps, ppr, rv, sv, d2,
    loc, locc, xa_s, xa_r, xc_s, xc_r, xl_s, xl_r,
    rr_s, rr_r, rl_s, rl_r, ga_r, gr_s, gl_s, pp_s, pp_r, st_s, st_r,
):
    me = lax.axis_index("rows")
    w = lax.axis_index("wide")
    k = me // 2
    p = me % 2
    other = 1 - w
    partner = k * 2 + (1 - p)
    right = jnp.minimum(k + 1, m - 1) * 2 + p
    left = jnp.maximum(k - 1, 0) * 2 + p
    mh = m // wides

    def remote(src, dst, ss, rs, **to):
        return pltpu.make_async_remote_copy(
            src_ref=src, dst_ref=dst, send_sem=ss, recv_sem=rs,
            device_id=to, device_id_type=MESH,
        )

    own_at = pltpu.make_async_copy(at_in.at[:, p], at2.at[:, :, pl.ds(0, tok)], loc.at[0])
    own_l = pltpu.make_async_copy(l2.at[p], lown, loc.at[1])
    own_r = pltpu.make_async_copy(r_in, rv, loc.at[2])

    def own_c(c):
        cols = pl.ds(pl.multiple_of(c * CW, CW), CW)
        return pltpu.make_async_copy(c_in.at[:, cols], cc.at[c, pl.ds(0, tok)], locc.at[c])

    half = pl.ds(w * mh, mh)
    ohalf = pl.ds(other * mh, mh)
    part = pl.ds(tok, tok)
    send_at = remote(
        at_in.at[half, 1 - p], at2.at[half, :, part], xa_s.at[0], xa_r.at[0], rows=partner)
    fwd_at = remote(
        at2.at[half, :, part], at2.at[half, :, part], xa_s.at[1], xa_r.at[1], wide=other)
    got_at = remote(
        at2.at[ohalf, :, part], at2.at[ohalf, :, part], xa_s.at[1], xa_r.at[1], wide=other)
    send_l = remote(l2.at[1 - p, w], lr.at[w], xl_s.at[0], xl_r.at[0], rows=partner)
    fwd_l = remote(lr.at[w], lr.at[w], xl_s.at[1], xl_r.at[1], wide=other)
    got_l = remote(lr.at[other], lr.at[other], xl_s.at[1], xl_r.at[1], wide=other)

    def send_c(c):
        cols = pl.ds(pl.multiple_of(c * CW, CW), CW)
        return remote(
            c_in.at[:, cols], cc.at[c, part], xc_s.at[c], xc_r.at[c], rows=partner)

    def rs_right(c, b):
        return remote(
            rbuf.at[c, b], rbuf.at[c, b], rr_s.at[c, b], rr_r.at[c, b], rows=right)

    def rs_left(c, b):
        return remote(lbuf.at[c, b], lbuf.at[c, b], rl_s.at[c, b], rl_r.at[c, b], rows=left)

    def block_rows(b):
        return pl.ds(pl.multiple_of(b * blk, blk), blk)

    def ag_right(c, b):
        ref = gbuf.at[c, block_rows(b)]
        return remote(ref, ref, gr_s.at[c, b], ga_r.at[c, b], rows=right)

    def ag_left(c, b):
        ref = gbuf.at[c, block_rows(b)]
        return remote(ref, ref, gl_s.at[c, b], ga_r.at[c, b], rows=left)

    def send_pp(c):
        return remote(pps.at[c], ppr.at[c], pp_s.at[c], pp_r.at[c], rows=partner)

    barrier = pltpu.get_barrier_semaphore()

    def greet(i, _):
        pl.semaphore_signal(
            barrier, inc=1, device_id={"rows": lax.rem(me + i, n)}, device_id_type=MESH)
        return 0

    own_at.start()
    lax.fori_loop(0, nc, lambda c, _: (own_c(c).start(), 0)[1], 0)
    lax.fori_loop(1, n, greet, 0)
    pl.semaphore_signal(barrier, inc=1, device_id={"wide": other}, device_id_type=MESH)
    pl.semaphore_wait(barrier, n)

    send_c(0).start()
    send_at.start()
    send_c(1).start()
    own_l.start()
    own_r.start()

    @pl.when(k == 0)
    def _():
        rbuf[...] = jnp.zeros_like(rbuf)

    @pl.when(k == m - 1)
    def _():
        lbuf[...] = jnp.zeros_like(lbuf)

    d2[...] = jnp.zeros_like(d2)
    pre[...] = jnp.zeros_like(pre)
    lax.fori_loop(0, nc, lambda c, _: (own_c(c).wait(), 0)[1], 0)
    own_at.wait()
    send_at.wait_recv()
    fwd_at.start()
    got_at.wait_recv()

    def term(c, b):
        return jnp.dot(at2[b], cc[c], preferred_element_type=F32)

    def reduce_step(c):
        @pl.when(c + 2 < nc)
        def _():
            send_c(c + 2).start()

        @pl.when(c == 0)
        def _():
            send_l.start()

        send_c(c).wait_recv()

        def far(i, _):
            d = m - 1 - i

            @pl.when(k + d < m)
            def _():
                b = k + d
                x = term(c, b)

                @pl.when(k > 0)
                def _():
                    rs_right(c, b).wait_recv()

                rbuf[c, b] = (x + rbuf[c, b].astype(F32)).astype(BF16)
                rs_right(c, b).start()

            @pl.when(k - d >= 0)
            def _():
                b = k - d
                x = term(c, b)

                @pl.when(k < m - 1)
                def _():
                    rs_left(c, b).wait_recv()

                lbuf[c, b] = (x + lbuf[c, b].astype(F32)).astype(BF16)
                rs_left(c, b).start()

            return 0

        lax.fori_loop(0, m - 1, far, 0)

    def own_step(c):
        x = term(c, k)

        @pl.when(k > 0)
        def _():
            rs_right(c, k).wait_recv()

        @pl.when(k < m - 1)
        def _():
            rs_left(c, k).wait_recv()

        g = x + rbuf[c, k].astype(F32) + lbuf[c, k].astype(F32)
        gbuf[c, block_rows(k)] = g.astype(BF16)

        @pl.when(k < m - 1)
        def _():
            ag_right(c, k).start()

        @pl.when(k > 0)
        def _():
            ag_left(c, k).start()

        cols = pl.ds(pl.multiple_of(c * CW, CW), CW)
        g_out[:, cols] = g
        new = BETA_TWO * second[:, cols] + (1.0 - BETA_TWO) * g * g
        direction = g / (jnp.sqrt(new) + GRAFT_EPS)
        d2[...] += jnp.sum((direction * direction).reshape(blk // 8, 8, CW), axis=0)

    def gather_step(c):
        def near(d, _):
            @pl.when(k - d >= 0)
            def _():
                ag_right(c, k - d).wait_recv()

                @pl.when(k < m - 1)
                def _():
                    ag_right(c, k - d).start()

            @pl.when(k + d < m)
            def _():
                ag_left(c, k + d).wait_recv()

                @pl.when(k > 0)
                def _():
                    ag_left(c, k + d).start()

            return 0

        lax.fori_loop(1, m, near, 0)

    def times(lref, c):
        kh = (m * blk) // wides
        x = jnp.dot(lref[0], gbuf[c, pl.ds(0, kh)], preferred_element_type=F32)
        for h in range(1, wides):
            x += jnp.dot(lref[h], gbuf[c, pl.ds(h * kh, kh)], preferred_element_type=F32)
        return x

    def left_step(c):
        @pl.when(c == 0)
        def _():
            own_l.wait()
            got_l.wait_recv()

        pps[c] = times(lr, c).astype(BF16)
        send_pp(c).start()

    def right_step(c):
        @pl.when(c == 0)
        def _():
            own_r.wait()

        x = times(lown, c)
        send_pp(c).wait_recv()
        x = (x + ppr[c].astype(F32)).astype(BF16)
        depth = pl.ds(pl.multiple_of(c * CW, CW), CW)

        def tile(j, _):
            cols = pl.ds(pl.multiple_of(j * CW, CW), CW)
            pre[:, cols] += jnp.dot(
                x, rv[depth, cols].astype(BF16), preferred_element_type=F32)
            return 0

        lax.fori_loop(0, nc, tile, 0)

    def step(t, _):
        @pl.when(t < nc)
        def _():
            reduce_step(t)

        @pl.when((t >= 1) & (t < nc + 1))
        def _():
            own_step(t - 1)

        @pl.when(t == 1)
        def _():
            send_l.wait_recv()
            fwd_l.start()

        @pl.when((t >= 2) & (t < nc + 2))
        def _():
            gather_step(t - 2)
            left_step(t - 2)

        @pl.when((t >= 3) & (t < nc + 3))
        def _():
            right_step(t - 3)

        return 0

    lax.fori_loop(0, nc + 3, step, 0)

    graft = jnp.sum(d2[...])
    x = pre[...]
    root = jnp.sum(x * x)
    rows8 = lax.broadcasted_iota(jnp.int32, (8, 128), 0)
    sv[me] = jnp.where(rows8 == 0, graft, root)

    def stat(peer, src):
        return remote(sv.at[src], sv.at[src], st_s.at[peer], st_r.at[src], rows=peer)

    def peer_of(i):
        return lax.rem(me + i, n)

    lax.fori_loop(1, n, lambda i, _: (stat(peer_of(i), me).start(), 0)[1], 0)

    def drain(c, _):
        send_c(c).wait_send()
        send_pp(c).wait_send()

        def each(b, _):
            @pl.when(b > k)
            def _():
                rs_right(c, b).wait_send()

            @pl.when(b < k)
            def _():
                rs_left(c, b).wait_send()

            @pl.when((b <= k) & (k < m - 1))
            def _():
                ag_right(c, b).wait_send()

            @pl.when((b >= k) & (k > 0))
            def _():
                ag_left(c, b).wait_send()

            return 0

        lax.fori_loop(0, m, each, 0)
        return 0

    lax.fori_loop(0, nc, drain, 0)
    send_at.wait_send()
    fwd_at.wait_send()
    send_l.wait_send()
    fwd_l.wait_send()
    lax.fori_loop(1, n, lambda i, _: (stat(peer_of(i), peer_of(i)).wait_recv(), 0)[1], 0)
    lax.fori_loop(1, n, lambda i, _: (stat(peer_of(i), me).wait_send(), 0)[1], 0)
    tot[...] = jnp.sum(sv[...], axis=0)


def per_device(n, wides, activations, cotangents, left_root, right_root, momentum, second_moment):
    tok, lb = activations.shape
    rb = cotangents.shape[1]
    blk = left_root.shape[0]
    m = n // 2
    nc = rb // CW
    kh = (m * blk) // wides
    at_in = activations.T.reshape(m, 2, blk, tok)
    l2 = (
        left_root.astype(BF16).reshape(blk, m, 2, blk).transpose(2, 0, 1, 3)
        .reshape(2, blk, wides, kh).transpose(0, 2, 1, 3)
    )
    anywhere = pl.BlockSpec(memory_space=pl.ANY)
    vmem = pl.BlockSpec(memory_space=pltpu.VMEM)
    dma = pltpu.SemaphoreType.DMA
    pre, gradient, tot = pl.pallas_call(
        functools.partial(kernel, n, wides, m, nc, blk, tok),
        out_shape=(
            jax.ShapeDtypeStruct((blk, rb), F32),
            jax.ShapeDtypeStruct((blk, rb), F32),
            jax.ShapeDtypeStruct((8, 128), F32),
        ),
        in_specs=[anywhere, anywhere, anywhere, anywhere, vmem],
        out_specs=(vmem, vmem, vmem),
        scratch_shapes=[
            pltpu.VMEM((m, blk, 2 * tok), BF16),
            pltpu.VMEM((nc, 2 * tok, CW), BF16),
            pltpu.VMEM((nc, m, blk, CW), BF16),
            pltpu.VMEM((nc, m, blk, CW), BF16),
            pltpu.VMEM((nc, m * blk, CW), BF16),
            pltpu.VMEM((wides, blk, kh), BF16),
            pltpu.VMEM((wides, blk, kh), BF16),
            pltpu.VMEM((nc, blk, CW), BF16),
            pltpu.VMEM((nc, blk, CW), BF16),
            pltpu.VMEM((rb, rb), F32),
            pltpu.VMEM((n, 8, 128), F32),
            pltpu.VMEM((8, CW), F32),
            dma((3,)), dma((nc,)), dma((2,)), dma((2,)), dma((nc,)), dma((nc,)),
            dma((2,)), dma((2,)),
            dma((nc, m)), dma((nc, m)), dma((nc, m)), dma((nc, m)),
            dma((nc, m)), dma((nc, m)), dma((nc, m)),
            dma((nc,)), dma((nc,)), dma((n,)), dma((n,)),
        ],
        compiler_params=pltpu.CompilerParams(
            collective_id=0, has_side_effects=True, vmem_limit_bytes=58 * 2**20,
        ),
    )(at_in, cotangents, l2, right_root[0], second_moment)
    new_second = BETA_TWO * second_moment + (1.0 - BETA_TWO) * gradient * gradient
    factor = jnp.sqrt(tot[0, 0]) / jnp.sqrt(tot[1, 0] + NORM_EPS)
    new_momentum = BETA_ONE * momentum + factor * pre
    return (new_momentum, new_second)


def solution(mesh):
    placed = (
        P(("groups", "rows"), None),
        P(("groups", "rows"), "wide"),
        P(("groups", "rows"), None),
        P(("groups", "wide"), None, None),
        P(("groups", "rows"), "wide"),
        P(("groups", "rows"), "wide"),
    )
    return jax.shard_map(
        functools.partial(per_device, mesh.shape["rows"], mesh.shape["wide"]),
        mesh=mesh,
        in_specs=placed,
        out_specs=(P(("groups", "rows"), "wide"), P(("groups", "rows"), "wide")),
        check_vma=False,
    )
```

time: 385 us -> 261 us (0.68)
  waiting for transfers between devices: 294 us -> 0 us
  Pallas kernels: 0 us -> 220 us
  matrix products: 45.8 us -> 0 us
  local copies, waits for them, and re-layouts: 1.27 us -> 30.2 us
  blocking collectives: 19.1 us -> 0 us
  between operations: 15.3 us -> 2.04 us
    pallas_call x0 -> x1, Pallas kernels: none -> 220 us  [per_device(): pl.pallas_call(functools.partial(kernel, n, wides, m, nc, blk, tok), out_...]
    reduce_scatter x1 -> x0, waiting for transfers between devices: 163 us -> none  [per_device(): lax.psum_scatter(lax.optimization_barrier(partial_term.astype(jnp.bfloat1...]
    all_gather x1 -> x0, waiting for transfers between devices: 131 us -> none  [per_device(): lax.all_gather(rounded_gradient, 'rows', axis=0, tiled=True)]
    dot_general x3 -> x0, matrix products: 45.8 us -> none  [the longest x1 21.1 us: per_device(): jnp.dot(left_root, lax.all_gather(rounded_gradient, 'rows', axis=0, tiled...]
    reshape x0 -> x3, local copies, waits for them, and re-layouts: none -> 23 us  [the longest x2 16.9 us: per_device(): left_root.astype(BF16).reshape(blk, m, 2, blk).transpose(2, 0, 1, 3)]
    psum x1 -> x0, blocking collectives: 19.1 us -> none  [per_device(): graft_total = lax.psum(graft_local, 'rows')]
    transpose x0 -> x1, local copies, waits for them, and re-layouts: none -> 5.91 us  [per_device(): at_in = activations.T.reshape(m, 2, blk, tok)]
    reduce_sum x1 -> x0, other arithmetic: 5.2 us -> none  [per_device(): graft_local = jnp.sum(direction * direction)]
  transfers between devices with their start and end apart: 2 -> 0, of which waited for: 2 -> 0; matrix products, arithmetic and copies ran while one was open for 1% -> 0% of each run, Pallas kernels for 0% -> 0%
where the time goes in v1:
time: 261 us
  Pallas kernels  220 us (84%)
  local copies, waits for them, and re-layouts  30.2 us (12%)
  other arithmetic  8.29 us (3%)
    pallas_call x1, Pallas kernels, per_device(): pl.pallas_call(functools.partial(kernel, n, wides, m, nc, blk, tok), out_...  220 us
    reshape x2, local copies, waits for them, and re-layouts, per_device(): left_root.astype(BF16).reshape(blk, m, 2, blk).transpose(2, 0, 1, 3)  16.9 us
    reshape x1, local copies, waits for them, and re-layouts, per_device(): l2 = left_root.astype(BF16).reshape(blk, m, 2, blk).transpose(2, 0, 1, 3)...  6.04 us
    transpose x1, local copies, waits for them, and re-layouts, per_device(): at_in = activations.T.reshape(m, 2, blk, tok)  5.91 us

profile of v1, /device:TPU:0, one launch (start us, length us, event | category | flops | bytes accessed | tf_op | source)
XLA Modules:
  0.0 260.5 jit_solution(3437314997511306046)
XLA Ops:
  0.6 3.2 %convert_element_type.3 = bf16[448,3584]{1,0:T(8,128)(2,1)S(1)} convert(f32[448,3584]{1,0:T(8,128)} %param.8) | non-fusion elementwise | flops 1605632 | bytes 9633792 | tf_op jit(solution)/shard_map/convert_element_type | solution.py:341
  3.8 5.9 %reshape.19 = bf16[448,4,2,448]{3,2,1,0:T(2,128)(2,1)} reshape(bf16[448,3584]{1,0:T(8,128)(2,1)S(1)} %convert_element_type.3) | data formatting | bytes 6422528 | tf_op jit(solution)/shard_map/reshape | solution.py:341
  9.7 11.1 %copy.10 = bf16[448,4,2,448]{0,3,1,2:T(8,128)(2,1)} copy(bf16[448,4,2,448]{3,2,1,0:T(2,128)(2,1)} %reshape.19) | data formatting | bytes 6422528 | tf_op jit(solution)/shard_map/reshape | solution.py:341
  20.7 6.0 %copy.11 = bf16[2,448,2,896]{3,1,2,0:T(8,128)(2,1)} copy(bf16[2,448,2,896]{1,3,2,0:T(8,128)(2,1)} %bitcast.8) | data formatting | bytes 6422528 | tf_op jit(solution)/shard_map/reshape | solution.py:342
  26.8 5.9 %copy.9 = bf16[3584,512]{1,0:T(8,128)(2,1)} copy(bf16[3584,512]{0,1:T(8,128)(2,1)} %bitcast.12) | data formatting | bytes 7340032 | tf_op jit(solution)/shard_map/transpose | solution.py:339
  32.7 0.0 copy-start
  32.7 0.0 copy-start.1
  32.7 220.0 %shard_map.77 = (f32[448,1280]{1,0:T(8,128)}, f32[448,1280]{1,0:T(8,128)}, f32[8,128]{1,0:T(8,128)}) custom-call(bf16[4,2,448,512]{3,2,1,0:T(8,128)(2,1)} %bitcast.9, bf16[512,1280]{1,0:T(8,128)(2,1)} %c_in.1, bf16[2,2,448,896]{3,2,1,0:T(8,128)(2,1)} %bitcast.10, f32[1280,1280]{1,0:T(8,128)} %bitcast.11, f32[448,1280]{1,0:T(8,128)} %second.1), custom_call_target="tpu_custom_call" | custom-call | tf_op jit(solution)/shard_map/pallas_call | solution.py:347
  252.7 1.3 fusion.1
  255.4 0.0 copy-done
  255.4 0.0 copy-done.1
  255.4 5.1 %fusion = (f32[448,1280]{1,0:T(8,128)}, f32[448,1280]{1,0:T(8,128)}) fusion(f32[448,1280]{1,0:T(8,128)} %get-tuple-element.7, f32[448,1280]{1,0:T(8,128)S(1)} %copy-done, f32[448,1280]{1,0:T(8,128)} %get-tuple-element.6, f32[]{:T(128)} %bitcast.6, f32[448,1280]{1,0:T(8,128)S(1)} %copy-done.1), kind=kLoop, calls=%fused_computation.1 | loop fusion | flops 4014080 | bytes 13762564 | tf_op jit(solution)/shard_map/add | solution.py:379
Async XLA Ops:
  32.7 222.7 %copy-start = (f32[448,1280]{1,0:T(8,128)S(1)}, f32[448,1280]{1,0:T(8,128)}, u32[]{:S(2)}) copy-start(f32[448,1280]{1,0:T(8,128)} %second.1) | copy-start | bytes 6881284
  32.7 222.7 %copy-start.1 = (f32[448,1280]{1,0:T(8,128)S(1)}, f32[448,1280]{1,0:T(8,128)}, u32[]{:S(2)}) copy-start(f32[448,1280]{1,0:T(8,128)} %param.10) | copy-start | bytes 6881284

commit v2 on v1

--- a/solution.py
+++ b/solution.py
@@ -1,4 +1,5 @@
 import functools
+import math
 
 import jax
 import jax.numpy as jnp
@@ -11,17 +12,17 @@
 BETA_TWO = 0.99
 GRAFT_EPS = 1e-08
 NORM_EPS = 1e-06
-CW = 256
+CW = 128
 MESH = pl.DeviceIdType.MESH
 F32 = jnp.float32
 BF16 = jnp.bfloat16
 
 
 def kernel(
-    n, wides, m, nc, blk, tok,
-    at_in, c_in, l2, r_in, second,
+    n, wides, m, nc, blk, tok, win,
+    at_in, c_in, l_in, r_in, second,
     pre, g_out, tot,
-    at2, cc, rbuf, lbuf, gbuf, lown, lr, pps, ppr, rv, sv, d2,
+    at2, cc, rbuf, lbuf, gbuf, lf, lown, ls, lr, pps, ppr, rv, sv, d2,
     loc, locc, xa_s, xa_r, xc_s, xc_r, xl_s, xl_r,
     rr_s, rr_r, rl_s, rl_r, ga_r, gr_s, gl_s, pp_s, pp_r, st_s, st_r,
 ):
@@ -42,7 +43,7 @@
         )
 
     own_at = pltpu.make_async_copy(at_in.at[:, p], at2.at[:, :, pl.ds(0, tok)], loc.at[0])
-    own_l = pltpu.make_async_copy(l2.at[p], lown, loc.at[1])
+    own_l = pltpu.make_async_copy(l_in, lf, loc.at[1])
     own_r = pltpu.make_async_copy(r_in, rv, loc.at[2])
 
     def own_c(c):
@@ -52,15 +53,49 @@
     half = pl.ds(w * mh, mh)
     ohalf = pl.ds(other * mh, mh)
     part = pl.ds(tok, tok)
-    send_at = remote(
-        at_in.at[half, 1 - p], at2.at[half, :, part], xa_s.at[0], xa_r.at[0], rows=partner)
-    fwd_at = remote(
-        at2.at[half, :, part], at2.at[half, :, part], xa_s.at[1], xa_r.at[1], wide=other)
-    got_at = remote(
-        at2.at[ohalf, :, part], at2.at[ohalf, :, part], xa_s.at[1], xa_r.at[1], wide=other)
-    send_l = remote(l2.at[1 - p, w], lr.at[w], xl_s.at[0], xl_r.at[0], rows=partner)
-    fwd_l = remote(lr.at[w], lr.at[w], xl_s.at[1], xl_r.at[1], wide=other)
-    got_l = remote(lr.at[other], lr.at[other], xl_s.at[1], xl_r.at[1], wide=other)
+    tw = tok // wides
+    part_w = pl.ds(pl.multiple_of(tok + w * tw, tw), tw)
+    part_o = pl.ds(pl.multiple_of(tok + other * tw, tw), tw)
+    token_w = pl.ds(pl.multiple_of(w * tw, tw), tw)
+
+    def send_at(b):
+        return remote(
+            at_in.at[b, 1 - p, :, token_w], at2.at[b, :, part_w], xa_s.at[0, b], xa_r.at[0, b],
+            rows=partner)
+
+    def fwd_at(b):
+        return remote(
+            at2.at[b, :, part_w], at2.at[b, :, part_w], xa_s.at[1, b], xa_r.at[1, b], wide=other)
+
+    def got_at(b):
+        return remote(
+            at2.at[b, :, part_o], at2.at[b, :, part_o], xa_s.at[1, b], xa_r.at[1, b], wide=other)
+
+    def far_first(f):
+        def both(i, _):
+            d = m - 1 - i
+
+            @pl.when(k + d < m)
+            def _():
+                f(k + d)
+
+            @pl.when(k - d >= 0)
+            def _():
+                f(k - d)
+
+            return 0
+
+        lax.fori_loop(0, m - 1, both, 0)
+        f(k)
+
+    def window(b, q):
+        first = (2 * b + q) * blk
+        start = jnp.minimum(first // 128 * 128, n * blk - win)
+        return pl.multiple_of(start, 128), first - start
+
+    send_l = remote(ls.at[half], lr.at[half], xl_s.at[0], xl_r.at[0], rows=partner)
+    fwd_l = remote(lr.at[half], lr.at[half], xl_s.at[1], xl_r.at[1], wide=other)
+    got_l = remote(lr.at[ohalf], lr.at[ohalf], xl_s.at[1], xl_r.at[1], wide=other)
 
     def send_c(c):
         cols = pl.ds(pl.multiple_of(c * CW, CW), CW)
@@ -75,7 +110,7 @@
         return remote(lbuf.at[c, b], lbuf.at[c, b], rl_s.at[c, b], rl_r.at[c, b], rows=left)
 
     def block_rows(b):
-        return pl.ds(pl.multiple_of(b * blk, blk), blk)
+        return pl.ds(pl.multiple_of(b * win + window(b, p)[1], 16), blk)
 
     def ag_right(c, b):
         ref = gbuf.at[c, block_rows(b)]
@@ -99,29 +134,45 @@
     lax.fori_loop(0, nc, lambda c, _: (own_c(c).start(), 0)[1], 0)
     lax.fori_loop(1, n, greet, 0)
     pl.semaphore_signal(barrier, inc=1, device_id={"wide": other}, device_id_type=MESH)
+    gbuf[...] = jnp.zeros_like(gbuf)
+
+    @pl.when(k == 0)
+    def _():
+        rbuf[...] = jnp.zeros_like(rbuf)
+
+    @pl.when(k == m - 1)
+    def _():
+        lbuf[...] = jnp.zeros_like(lbuf)
+
     pl.semaphore_wait(barrier, n)
 
     send_c(0).start()
-    send_at.start()
+    far_first(lambda b: send_at(b).start())
     send_c(1).start()
     own_l.start()
     own_r.start()
-
-    @pl.when(k == 0)
-    def _():
-        rbuf[...] = jnp.zeros_like(rbuf)
-
-    @pl.when(k == m - 1)
-    def _():
-        lbuf[...] = jnp.zeros_like(lbuf)
-
     d2[...] = jnp.zeros_like(d2)
     pre[...] = jnp.zeros_like(pre)
-    lax.fori_loop(0, nc, lambda c, _: (own_c(c).wait(), 0)[1], 0)
     own_at.wait()
-    send_at.wait_recv()
-    fwd_at.start()
-    got_at.wait_recv()
+
+    def arrive(c, b):
+        @pl.when(c == 0)
+        def _():
+            send_at(b).wait_recv()
+            fwd_at(b).start()
+            got_at(b).wait_recv()
+
+    def cast_left():
+        own_l.wait()
+
+        def one(b, _):
+            mine, _ = window(b, p)
+            theirs, _ = window(b, 1 - p)
+            ls[b] = lf[:, pl.ds(theirs, win)].astype(BF16)
+            lown[b] = lf[:, pl.ds(mine, win)].astype(BF16)
+            return 0
+
+        lax.fori_loop(0, m, one, 0)
 
     def term(c, b):
         return jnp.dot(at2[b], cc[c], preferred_element_type=F32)
@@ -131,10 +182,7 @@
         def _():
             send_c(c + 2).start()
 
-        @pl.when(c == 0)
-        def _():
-            send_l.start()
-
+        own_c(c).wait()
         send_c(c).wait_recv()
 
         def far(i, _):
@@ -143,6 +191,7 @@
             @pl.when(k + d < m)
             def _():
                 b = k + d
+                arrive(c, b)
                 x = term(c, b)
 
                 @pl.when(k > 0)
@@ -155,6 +204,7 @@
             @pl.when(k - d >= 0)
             def _():
                 b = k - d
+                arrive(c, b)
                 x = term(c, b)
 
                 @pl.when(k < m - 1)
@@ -167,6 +217,12 @@
             return 0
 
         lax.fori_loop(0, m - 1, far, 0)
+        arrive(c, k)
+
+        @pl.when(c == 0)
+        def _():
+            cast_left()
+            send_l.start()
 
     def own_step(c):
         x = term(c, k)
@@ -219,16 +275,14 @@
         lax.fori_loop(1, m, near, 0)
 
     def times(lref, c):
-        kh = (m * blk) // wides
-        x = jnp.dot(lref[0], gbuf[c, pl.ds(0, kh)], preferred_element_type=F32)
-        for h in range(1, wides):
-            x += jnp.dot(lref[h], gbuf[c, pl.ds(h * kh, kh)], preferred_element_type=F32)
+        x = jnp.dot(lref[0], gbuf[c, pl.ds(0, win)], preferred_element_type=F32)
+        for b in range(1, m):
+            x += jnp.dot(lref[b], gbuf[c, pl.ds(b * win, win)], preferred_element_type=F32)
         return x
 
     def left_step(c):
         @pl.when(c == 0)
         def _():
-            own_l.wait()
             got_l.wait_recv()
 
         pps[c] = times(lr, c).astype(BF16)
@@ -245,12 +299,12 @@
         depth = pl.ds(pl.multiple_of(c * CW, CW), CW)
 
         def tile(j, _):
-            cols = pl.ds(pl.multiple_of(j * CW, CW), CW)
+            cols = pl.ds(pl.multiple_of(j * 256, 256), 256)
             pre[:, cols] += jnp.dot(
                 x, rv[depth, cols].astype(BF16), preferred_element_type=F32)
             return 0
 
-        lax.fori_loop(0, nc, tile, 0)
+        lax.fori_loop(0, pre.shape[1] // 256, tile, 0)
 
     def step(t, _):
         @pl.when(t < nc)
@@ -298,6 +352,11 @@
         send_pp(c).wait_send()
 
         def each(b, _):
+            @pl.when(c == 0)
+            def _():
+                send_at(b).wait_send()
+                fwd_at(b).wait_send()
+
             @pl.when(b > k)
             def _():
                 rs_right(c, b).wait_send()
@@ -320,8 +379,6 @@
         return 0
 
     lax.fori_loop(0, nc, drain, 0)
-    send_at.wait_send()
-    fwd_at.wait_send()
     send_l.wait_send()
     fwd_l.wait_send()
     lax.fori_loop(1, n, lambda i, _: (stat(peer_of(i), peer_of(i)).wait_recv(), 0)[1], 0)
@@ -335,17 +392,13 @@
     blk = left_root.shape[0]
     m = n // 2
     nc = rb // CW
-    kh = (m * blk) // wides
+    win = -(-(blk + 128 - math.gcd(blk, 128)) // 128) * 128
     at_in = activations.T.reshape(m, 2, blk, tok)
-    l2 = (
-        left_root.astype(BF16).reshape(blk, m, 2, blk).transpose(2, 0, 1, 3)
-        .reshape(2, blk, wides, kh).transpose(0, 2, 1, 3)
-    )
     anywhere = pl.BlockSpec(memory_space=pl.ANY)
     vmem = pl.BlockSpec(memory_space=pltpu.VMEM)
     dma = pltpu.SemaphoreType.DMA
     pre, gradient, tot = pl.pallas_call(
-        functools.partial(kernel, n, wides, m, nc, blk, tok),
+        functools.partial(kernel, n, wides, m, nc, blk, tok, win),
         out_shape=(
             jax.ShapeDtypeStruct((blk, rb), F32),
             jax.ShapeDtypeStruct((blk, rb), F32),
@@ -358,15 +411,17 @@
             pltpu.VMEM((nc, 2 * tok, CW), BF16),
             pltpu.VMEM((nc, m, blk, CW), BF16),
             pltpu.VMEM((nc, m, blk, CW), BF16),
-            pltpu.VMEM((nc, m * blk, CW), BF16),
-            pltpu.VMEM((wides, blk, kh), BF16),
-            pltpu.VMEM((wides, blk, kh), BF16),
+            pltpu.VMEM((nc, m * win, CW), BF16),
+            pltpu.VMEM((blk, n * blk), F32),
+            pltpu.VMEM((m, blk, win), BF16),
+            pltpu.VMEM((m, blk, win), BF16),
+            pltpu.VMEM((m, blk, win), BF16),
             pltpu.VMEM((nc, blk, CW), BF16),
             pltpu.VMEM((nc, blk, CW), BF16),
             pltpu.VMEM((rb, rb), F32),
             pltpu.VMEM((n, 8, 128), F32),
             pltpu.VMEM((8, CW), F32),
-            dma((3,)), dma((nc,)), dma((2,)), dma((2,)), dma((nc,)), dma((nc,)),
+            dma((3,)), dma((nc,)), dma((2, m)), dma((2, m)), dma((nc,)), dma((nc,)),
             dma((2,)), dma((2,)),
             dma((nc, m)), dma((nc, m)), dma((nc, m)), dma((nc, m)),
             dma((nc, m)), dma((nc, m)), dma((nc, m)),
@@ -375,7 +430,7 @@
         compiler_params=pltpu.CompilerParams(
             collective_id=0, has_side_effects=True, vmem_limit_bytes=58 * 2**20,
         ),
-    )(at_in, cotangents, l2, right_root[0], second_moment)
+    )(at_in, cotangents, left_root, right_root[0], second_moment)
     new_second = BETA_TWO * second_moment + (1.0 - BETA_TWO) * gradient * gradient
     factor = jnp.sqrt(tot[0, 0]) / jnp.sqrt(tot[1, 0] + NORM_EPS)
     new_momentum = BETA_ONE * momentum + factor * pre

time: 261 us -> 281 us (1.077)
  Pallas kernels: 220 us -> 266 us
  local copies, waits for them, and re-layouts: 30.2 us -> 7.2 us
  other arithmetic: 8.29 us -> 5.13 us
    pallas_call x1, Pallas kernels: 220 us -> 266 us  [per_device(): pl.pallas_call(functools.partial(kernel, n, wides, m, nc, blk, tok, win),...]
    reshape x3 -> x0, local copies, waits for them, and re-layouts: 23 us -> none  [the longest x2 16.9 us: per_device(): left_root.astype(BF16).reshape(blk, m, 2, blk).transpose(2, 0, 1, 3)]
    convert_element_type x1 -> x0, other arithmetic: 3.16 us -> none  [per_device(): left_root.astype(BF16).reshape(blk, m, 2, blk).transpose(2, 0, 1, 3)]
where the time goes in v2:
time: 281 us; the launch traced here: 280 us
  Pallas kernels  266 us (95%)
  local copies, waits for them, and re-layouts  7.2 us (3%)
  other arithmetic  5.13 us (2%)
    pallas_call x1, Pallas kernels, per_device(): pl.pallas_call(functools.partial(kernel, n, wides, m, nc, blk, tok, win),...  266 us
    transpose x1, local copies, waits for them, and re-layouts, per_device(): at_in = activations.T.reshape(m, 2, blk, tok)  5.92 us

profile of v2, /device:TPU:0, one launch (start us, length us, event | category | flops | bytes accessed | tf_op | source)
XLA Modules:
  0.0 280.4 jit_solution(6690729805633958736)
XLA Ops:
  0.6 5.9 %copy.8 = bf16[3584,512]{1,0:T(8,128)(2,1)} copy(bf16[3584,512]{0,1:T(8,128)(2,1)} %bitcast.6) | data formatting | bytes 7340032 | tf_op jit(solution)/shard_map/transpose | solution.py:396
  6.6 0.0 copy-start
  6.6 0.0 copy-start.1
  6.6 266.0 %shard_map.77 = (f32[448,1280]{1,0:T(8,128)}, f32[448,1280]{1,0:T(8,128)}, f32[8,128]{1,0:T(8,128)}) custom-call(bf16[4,2,448,512]{3,2,1,0:T(8,128)(2,1)} %bitcast.4, bf16[512,1280]{1,0:T(8,128)(2,1)} %c_in.1, f32[448,3584]{1,0:T(8,128)} %l_in.1, f32[1280,1280]{1,0:T(8,128)} %bitcast.5, f32[448,1280]{1,0:T(8,128)} %second.1), custom_call_target="tpu_custom_call" | custom-call | tf_op jit(solution)/shard_map/pallas_call | solution.py:400
  272.6 1.3 fusion.1
  275.2 0.0 copy-done
  275.3 0.0 copy-done.1
  275.3 5.1 %fusion = (f32[448,1280]{1,0:T(8,128)}, f32[448,1280]{1,0:T(8,128)}) fusion(f32[448,1280]{1,0:T(8,128)} %get-tuple-element.7, f32[448,1280]{1,0:T(8,128)S(1)} %copy-done, f32[448,1280]{1,0:T(8,128)} %get-tuple-element.6, f32[]{:T(128)} %bitcast.3, f32[448,1280]{1,0:T(8,128)S(1)} %copy-done.1), kind=kLoop, calls=%fused_computation.1 | loop fusion | flops 4014080 | bytes 13762564 | tf_op jit(solution)/shard_map/add | solution.py:434
Async XLA Ops:
  6.6 268.7 %copy-start = (f32[448,1280]{1,0:T(8,128)S(1)}, f32[448,1280]{1,0:T(8,128)}, u32[]{:S(2)}) copy-start(f32[448,1280]{1,0:T(8,128)} %second.1) | copy-start | bytes 6881284
  6.6 268.7 %copy-start.1 = (f32[448,1280]{1,0:T(8,128)S(1)}, f32[448,1280]{1,0:T(8,128)}, u32[]{:S(2)}) copy-start(f32[448,1280]{1,0:T(8,128)} %param.10) | copy-start | bytes 6881284

commit v3 on v2

--- a/solution.py
+++ b/solution.py
@@ -177,7 +177,7 @@
     def term(c, b):
         return jnp.dot(at2[b], cc[c], preferred_element_type=F32)
 
-    def reduce_step(c):
+    def chunk_step(c):
         @pl.when(c + 2 < nc)
         def _():
             send_c(c + 2).start()
@@ -185,46 +185,39 @@
         own_c(c).wait()
         send_c(c).wait_recv()
 
-        def far(i, _):
-            d = m - 1 - i
-
-            @pl.when(k + d < m)
-            def _():
-                b = k + d
-                arrive(c, b)
-                x = term(c, b)
-
-                @pl.when(k > 0)
-                def _():
-                    rs_right(c, b).wait_recv()
-
-                rbuf[c, b] = (x + rbuf[c, b].astype(F32)).astype(BF16)
-                rs_right(c, b).start()
-
-            @pl.when(k - d >= 0)
-            def _():
-                b = k - d
-                arrive(c, b)
-                x = term(c, b)
-
-                @pl.when(k < m - 1)
-                def _():
-                    rs_left(c, b).wait_recv()
-
-                lbuf[c, b] = (x + lbuf[c, b].astype(F32)).astype(BF16)
-                rs_left(c, b).start()
-
-            return 0
-
-        lax.fori_loop(0, m - 1, far, 0)
+    def right_pass(c):
+        def one(i, _):
+            b = m - 1 - i
+            arrive(c, b)
+            x = term(c, b)
+
+            @pl.when(k > 0)
+            def _():
+                rs_right(c, b).wait_recv()
+
+            rbuf[c, b] = (x + rbuf[c, b].astype(F32)).astype(BF16)
+            rs_right(c, b).start()
+            return 0
+
+        lax.fori_loop(0, m - 1 - k, one, 0)
+
+    def left_pass(c):
+        def one(b, _):
+            arrive(c, b)
+            x = term(c, b)
+
+            @pl.when(k < m - 1)
+            def _():
+                rs_left(c, b).wait_recv()
+
+            lbuf[c, b] = (x + lbuf[c, b].astype(F32)).astype(BF16)
+            rs_left(c, b).start()
+            return 0
+
+        lax.fori_loop(0, k, one, 0)
+
+    def own_step(c):
         arrive(c, k)
-
-        @pl.when(c == 0)
-        def _():
-            cast_left()
-            send_l.start()
-
-    def own_step(c):
         x = term(c, k)
 
         @pl.when(k > 0)
@@ -252,23 +245,32 @@
         direction = g / (jnp.sqrt(new) + GRAFT_EPS)
         d2[...] += jnp.sum((direction * direction).reshape(blk // 8, 8, CW), axis=0)
 
-    def gather_step(c):
+    def own_lag(j):
+        return jnp.maximum(j, m - 1 - j)
+
+    def gather_step(t):
         def near(d, _):
-            @pl.when(k - d >= 0)
-            def _():
-                ag_right(c, k - d).wait_recv()
+            below = k - d
+            c_low = t - own_lag(below) - d
+
+            @pl.when((below >= 0) & (c_low >= 0) & (c_low < nc))
+            def _():
+                ag_right(c_low, below).wait_recv()
 
                 @pl.when(k < m - 1)
                 def _():
-                    ag_right(c, k - d).start()
-
-            @pl.when(k + d < m)
-            def _():
-                ag_left(c, k + d).wait_recv()
+                    ag_right(c_low, below).start()
+
+            above = k + d
+            c_high = t - own_lag(above) - d
+
+            @pl.when((above < m) & (c_high >= 0) & (c_high < nc))
+            def _():
+                ag_left(c_high, above).wait_recv()
 
                 @pl.when(k > 0)
                 def _():
-                    ag_left(c, k + d).start()
+                    ag_left(c_high, above).start()
 
             return 0
 
@@ -281,10 +283,6 @@
         return x
 
     def left_step(c):
-        @pl.when(c == 0)
-        def _():
-            got_l.wait_recv()
-
         pps[c] = times(lr, c).astype(BF16)
         send_pp(c).start()
 
@@ -306,32 +304,40 @@
 
         lax.fori_loop(0, pre.shape[1] // 256, tile, 0)
 
+    first_lag = jnp.minimum(k, m - 1 - k)
+    left_lag = m - 1 + own_lag(k)
+
+    def at_lag(t, lag, f):
+        @pl.when((t >= lag) & (t < nc + lag))
+        def _():
+            f(t - lag)
+
     def step(t, _):
-        @pl.when(t < nc)
-        def _():
-            reduce_step(t)
-
-        @pl.when((t >= 1) & (t < nc + 1))
-        def _():
-            own_step(t - 1)
-
-        @pl.when(t == 1)
+        at_lag(t, first_lag, chunk_step)
+        at_lag(t, k, right_pass)
+        at_lag(t, m - 1 - k, left_pass)
+        at_lag(t, own_lag(k), own_step)
+        gather_step(t)
+
+        @pl.when(t == 0)
+        def _():
+            cast_left()
+            send_l.start()
+
+        @pl.when(t == left_lag - 1)
         def _():
             send_l.wait_recv()
             fwd_l.start()
 
-        @pl.when((t >= 2) & (t < nc + 2))
-        def _():
-            gather_step(t - 2)
-            left_step(t - 2)
-
-        @pl.when((t >= 3) & (t < nc + 3))
-        def _():
-            right_step(t - 3)
-
+        @pl.when(t == left_lag)
+        def _():
+            got_l.wait_recv()
+
+        at_lag(t, left_lag, left_step)
+        at_lag(t, left_lag + 1, right_step)
         return 0
 
-    lax.fori_loop(0, nc + 3, step, 0)
+    lax.fori_loop(0, nc + left_lag + 1, step, 0)
 
     graft = jnp.sum(d2[...])
     x = pre[...]

time: 281 us -> 189 us (0.67)
  Pallas kernels: 266 us -> 175 us
    pallas_call x1, Pallas kernels: 266 us -> 175 us  [per_device(): pl.pallas_call(functools.partial(kernel, n, wides, m, nc, blk, tok, win),...]
where the time goes in v3:
time: 189 us
  Pallas kernels  175 us (93%)
  local copies, waits for them, and re-layouts  7.2 us (4%)
  other arithmetic  5.13 us (3%)
  between operations  2.04 us (1%)
    pallas_call x1, Pallas kernels, per_device(): pl.pallas_call(functools.partial(kernel, n, wides, m, nc, blk, tok, win),...  175 us
    transpose x1, local copies, waits for them, and re-layouts, per_device(): at_in = activations.T.reshape(m, 2, blk, tok)  5.92 us
    add x1, other arithmetic, per_device(): BETA_TWO * second_moment + (1.0 - BETA_TWO) * gradient * gradient  5.13 us

profile of v3, /device:TPU:0, one launch (start us, length us, event | category | flops | bytes accessed | tf_op | source)
XLA Modules:
  0.0 189.2 jit_solution(10913873413425493780)
XLA Ops:
  0.6 5.9 %copy.8 = bf16[3584,512]{1,0:T(8,128)(2,1)} copy(bf16[3584,512]{0,1:T(8,128)(2,1)} %bitcast.6) | data formatting | bytes 7340032 | tf_op jit(solution)/shard_map/transpose | solution.py:402
  6.6 0.0 copy-start
  6.6 0.0 copy-start.1
  6.6 174.8 %shard_map.77 = (f32[448,1280]{1,0:T(8,128)}, f32[448,1280]{1,0:T(8,128)}, f32[8,128]{1,0:T(8,128)}) custom-call(bf16[4,2,448,512]{3,2,1,0:T(8,128)(2,1)} %bitcast.4, bf16[512,1280]{1,0:T(8,128)(2,1)} %c_in.1, f32[448,3584]{1,0:T(8,128)} %l_in.1, f32[1280,1280]{1,0:T(8,128)} %bitcast.5, f32[448,1280]{1,0:T(8,128)} %second.1), custom_call_target="tpu_custom_call" | custom-call | tf_op jit(solution)/shard_map/pallas_call | solution.py:406
  181.4 1.3 fusion.1
  184.1 0.0 copy-done
  184.1 0.0 copy-done.1
  184.1 5.1 %fusion = (f32[448,1280]{1,0:T(8,128)}, f32[448,1280]{1,0:T(8,128)}) fusion(f32[448,1280]{1,0:T(8,128)} %get-tuple-element.7, f32[448,1280]{1,0:T(8,128)S(1)} %copy-done, f32[448,1280]{1,0:T(8,128)} %get-tuple-element.6, f32[]{:T(128)} %bitcast.3, f32[448,1280]{1,0:T(8,128)S(1)} %copy-done.1), kind=kLoop, calls=%fused_computation.1 | loop fusion | flops 4014080 | bytes 13762564 | tf_op jit(solution)/shard_map/add | solution.py:440
Async XLA Ops:
  6.6 177.5 %copy-start = (f32[448,1280]{1,0:T(8,128)S(1)}, f32[448,1280]{1,0:T(8,128)}, u32[]{:S(2)}) copy-start(f32[448,1280]{1,0:T(8,128)} %second.1) | copy-start | bytes 6881284
  6.6 177.5 %copy-start.1 = (f32[448,1280]{1,0:T(8,128)S(1)}, f32[448,1280]{1,0:T(8,128)}, u32[]{:S(2)}) copy-start(f32[448,1280]{1,0:T(8,128)} %param.10) | copy-start | bytes 6881284

commit v4 on v3

--- a/solution.py
+++ b/solution.py
@@ -148,7 +148,8 @@
 
     send_c(0).start()
     far_first(lambda b: send_at(b).start())
-    send_c(1).start()
+    for ahead in range(1, min(4, nc)):
+        send_c(ahead).start()
     own_l.start()
     own_r.start()
     d2[...] = jnp.zeros_like(d2)
@@ -178,9 +179,9 @@
         return jnp.dot(at2[b], cc[c], preferred_element_type=F32)
 
     def chunk_step(c):
-        @pl.when(c + 2 < nc)
-        def _():
-            send_c(c + 2).start()
+        @pl.when(c + 4 < nc)
+        def _():
+            send_c(c + 4).start()
 
         own_c(c).wait()
         send_c(c).wait_recv()
@@ -319,7 +320,7 @@
         at_lag(t, own_lag(k), own_step)
         gather_step(t)
 
-        @pl.when(t == 0)
+        @pl.when(t == 1)
         def _():
             cast_left()
             send_l.start()

time: 189 us -> 179 us (0.947)
  Pallas kernels: 175 us -> 164 us
    pallas_call x1, Pallas kernels: 175 us -> 164 us  [per_device(): pl.pallas_call(functools.partial(kernel, n, wides, m, nc, blk, tok, win),...]
where the time goes in v4:
time: 179 us
  Pallas kernels  164 us (92%)
  local copies, waits for them, and re-layouts  7.2 us (4%)
  other arithmetic  5.13 us (3%)
  between operations  2.04 us (1%)
    pallas_call x1, Pallas kernels, per_device(): pl.pallas_call(functools.partial(kernel, n, wides, m, nc, blk, tok, win),...  164 us
    transpose x1, local copies, waits for them, and re-layouts, per_device(): at_in = activations.T.reshape(m, 2, blk, tok)  5.92 us
    add x1, other arithmetic, per_device(): BETA_TWO * second_moment + (1.0 - BETA_TWO) * gradient * gradient  5.13 us

profile of v4, /device:TPU:0, one launch (start us, length us, event | category | flops | bytes accessed | tf_op | source)
XLA Modules:
  0.0 178.6 jit_solution(7645361596985696679)
XLA Ops:
  0.6 5.9 %copy.8 = bf16[3584,512]{1,0:T(8,128)(2,1)} copy(bf16[3584,512]{0,1:T(8,128)(2,1)} %bitcast.6) | data formatting | bytes 7340032 | tf_op jit(solution)/shard_map/transpose | solution.py:403
  6.6 0.0 copy-start
  6.6 0.0 copy-start.1
  6.6 164.2 %shard_map.77 = (f32[448,1280]{1,0:T(8,128)}, f32[448,1280]{1,0:T(8,128)}, f32[8,128]{1,0:T(8,128)}) custom-call(bf16[4,2,448,512]{3,2,1,0:T(8,128)(2,1)} %bitcast.4, bf16[512,1280]{1,0:T(8,128)(2,1)} %c_in.1, f32[448,3584]{1,0:T(8,128)} %l_in.1, f32[1280,1280]{1,0:T(8,128)} %bitcast.5, f32[448,1280]{1,0:T(8,128)} %second.1), custom_call_target="tpu_custom_call" | custom-call | tf_op jit(solution)/shard_map/pallas_call | solution.py:407
  170.8 1.3 fusion.1
  173.5 0.0 copy-done
  173.5 0.0 copy-done.1
  173.5 5.1 %fusion = (f32[448,1280]{1,0:T(8,128)}, f32[448,1280]{1,0:T(8,128)}) fusion(f32[448,1280]{1,0:T(8,128)} %get-tuple-element.7, f32[448,1280]{1,0:T(8,128)S(1)} %copy-done, f32[448,1280]{1,0:T(8,128)} %get-tuple-element.6, f32[]{:T(128)} %bitcast.3, f32[448,1280]{1,0:T(8,128)S(1)} %copy-done.1), kind=kLoop, calls=%fused_computation.1 | loop fusion | flops 4014080 | bytes 13762564 | tf_op jit(solution)/shard_map/add | solution.py:441
Async XLA Ops:
  6.6 166.9 %copy-start = (f32[448,1280]{1,0:T(8,128)S(1)}, f32[448,1280]{1,0:T(8,128)}, u32[]{:S(2)}) copy-start(f32[448,1280]{1,0:T(8,128)} %second.1) | copy-start | bytes 6881284
  6.6 166.9 %copy-start.1 = (f32[448,1280]{1,0:T(8,128)S(1)}, f32[448,1280]{1,0:T(8,128)}, u32[]{:S(2)}) copy-start(f32[448,1280]{1,0:T(8,128)} %param.10) | copy-start | bytes 6881284
